TPU v7x, 32 devices: a whole 2x2x4 slice. The times are simulated.
32 devices in a mesh: groups: 2 (over y), seq: 4 (over z), dp: 4 (over x, core).
Axes of the slice: x: 2, y: 2, z: 4, core: 2. Of those that a mesh axis runs over, the one named last changes fastest.
Arguments:
- inputs: bfloat16 [8, 65536, 512], P(('groups', 'dp'), 'seq'), parts along dimension 0, may hold values from -6 to 6
- cotangent: bfloat16 [8, 65536, 512], P(('groups', 'dp'), 'seq'), parts along dimension 0, may hold values from -6 to 6
- first_factor: bfloat16 [256, 256, 256], P('seq', 'dp'), may hold values from -0.375 to 0.375
- second_factor: bfloat16 [256, 256, 256], P('seq', 'dp'), may hold values from -0.375 to 0.375
Outputs:
- mixed_out: bfloat16 [8, 65536, 512], P(('groups', 'dp'), 'seq'), parts along dimension 0
- input_grad: bfloat16 [8, 65536, 512], P(('groups', 'dp'), 'seq'), parts along dimension 0
- first_factor_grad: bfloat16 [512, 256, 256], P(('groups', 'seq'), 'dp'), parts along dimension 0
- second_factor_grad: bfloat16 [512, 256, 256], P(('groups', 'seq'), 'dp'), parts along dimension 0
There are 2 independent parts, one for each index of `groups`. A program takes and returns all parts, laid end to end along the dimension named above; an argument that names none is the same for every part. Nothing has to cross between parts.
All inputs are finite; a program needn't handle non-finite values.
Results may differ from a plain program's by a relative error of at most 0.009.
Values may be sent and summed in bfloat16 or wider, within the bound.
A program may use at most 320 MiB of HBM per device.

v0:
```python
import math
import jax
import jax.numpy as jnp
from jax import lax
from jax.sharding import PartitionSpec as P


def silu_parts(values):
    sig = jax.nn.sigmoid(values)
    return (values * sig, sig * (1.0 + values * (1.0 - sig)))


def shards(inputs, cotangent, first_factor, second_factor):
    first_full, second_full = (
        lax.all_gather(first_factor, "dp", axis=1, tiled=True),
        lax.all_gather(second_factor, "dp", axis=1, tiled=True),
    )
    seqs_here = inputs.shape[0]
    rows_here = inputs.shape[1]
    channels = inputs.shape[2]
    blocks_here = first_full.shape[0]
    block_width = first_full.shape[1]
    columns_here = second_full.shape[0]
    second_width = second_full.shape[1]
    norm_scale = 1.0 / math.sqrt(lax.axis_size("dp") * seqs_here * channels)
    blocked = inputs.reshape(seqs_here, blocks_here, block_width, channels)
    first_out = jnp.einsum(
        "ijk,bikc->bijc", first_full, blocked, preferred_element_type=jnp.float32
    ).astype(jnp.bfloat16)
    exchanged = lax.all_to_all(first_out, "seq", split_axis=2, concat_axis=1, tiled=True)
    result = jnp.einsum(
        "jik,bkjc->bjic", second_full, exchanged, preferred_element_type=jnp.float32
    )
    mixing, exchanged = (result, exchanged)
    mixing = mixing.reshape(seqs_here, rows_here, channels)
    gate_value, gate_slope = silu_parts(inputs.astype(jnp.float32))
    outputs = (mixing * gate_value).astype(jnp.bfloat16)
    cot_f32 = cotangent.astype(jnp.float32)
    gated_cot = (
        (cot_f32 * gate_value)
        .astype(jnp.bfloat16)
        .reshape(seqs_here, columns_here, second_width, channels)
    )
    grad_two = norm_scale * jnp.einsum(
        "bjic,bkjc->jik", gated_cot, exchanged, preferred_element_type=jnp.float32
    )
    back_sent = jnp.einsum(
        "jik,bjic->bkjc", second_full, gated_cot, preferred_element_type=jnp.float32
    ).astype(jnp.bfloat16)
    back_rows = lax.all_to_all(back_sent, "seq", split_axis=1, concat_axis=2, tiled=True)
    grad_one = norm_scale * jnp.einsum(
        "bijc,bikc->ijk", back_rows, blocked, preferred_element_type=jnp.float32
    )
    local_grad = jnp.einsum(
        "ijk,bijc->bikc", first_full, back_rows, preferred_element_type=jnp.float32
    )
    input_grad = (
        local_grad.reshape(seqs_here, rows_here, channels) + cot_f32 * mixing * gate_slope
    ).astype(jnp.bfloat16)
    first_sum, second_sum = (
        lax.psum_scatter(
            grad_one.astype(jnp.bfloat16), "dp", scatter_dimension=1, tiled=True
        ).astype(jnp.float32),
        lax.psum_scatter(
            grad_two.astype(jnp.bfloat16), "dp", scatter_dimension=1, tiled=True
        ).astype(jnp.float32),
    )
    return (outputs, input_grad, first_sum.astype(jnp.bfloat16), second_sum.astype(jnp.bfloat16))


def solution(mesh):
    in_specs = (
        P(("groups", "dp"), "seq", None),
        P(("groups", "dp"), "seq", None),
        P("seq", "dp", None),
        P("seq", "dp", None),
    )
    out_specs = (
        P(("groups", "dp"), "seq", None),
        P(("groups", "dp"), "seq", None),
        P(("groups", "seq"), "dp", None),
        P(("groups", "seq"), "dp", None),
    )
    return jax.shard_map(shards, mesh=mesh, in_specs=in_specs, out_specs=out_specs, check_vma=False)
```

profile of v0, /device:TPU:0, one launch (start us, length us, event | category | flops | bytes accessed | tf_op | source)
XLA Modules:
  0.0 976.6 jit_solution(17166616666703134738)
XLA Ops:
  7.2 0.0 all-gather.3.cloned.1.call-start
  7.2 0.7 all-gather.3.cloned.1.call-update
  7.9 62.7 %all-gather.3.cloned.1.call-done = bf16[64,256,256]{2,1,0:T(8,128)(2,1)} async-done(((bf16[64,64,256]{2,1,0:T(8,128)(2,1)}), bf16[64,256,256]{2,1,0:T(8,128)(2,1)}) %all-gather.3.cloned.1.call-update) | async-done | bytes 8388624 | tf_op jit(solution)/shard_map/all_gather | solution.py:15
  70.6 19.3 %convert_bitcast_fusion.1 = bf16[1,64,256,512]{2,3,1,0:T(8,128)(2,1)} fusion(bf16[64,256,512]{2,1,0:T(8,128)(2,1)} %bitcast.45, bf16[64,256,256]{2,1,0:T(8,128)(2,1)} %all-gather.3.cloned.1.call-done), kind=kOutput, calls=%fused_computation.19 | convolution fusion | flops 4303355904 | bytes 41943040 | tf_op jit(solution)/shard_map/ijk,bikc->bijc/dot_general | solution.py:27
  89.9 23.4 %copy.19 = bf16[1,64,256,512]{3,1,0,2:T(8,128)(2,1)} copy(bf16[1,64,256,512]{2,3,1,0:T(8,128)(2,1)} %convert_bitcast_fusion.1) | data formatting | bytes 33554432 | tf_op jit(solution)/shard_map/convert_element_type | solution.py:29
  113.3 7.0 all-to-all-start
  120.3 0.0 all-gather.5.cloned.1.call-start
  120.3 0.7 all-gather.5.cloned.1.call-update
  121.0 22.1 %fusion = bf16[1,16384,512]{2,1,0:T(8,128)(2,1)} fusion(bf16[1,16384,512]{2,1,0:T(8,128)(2,1)} %param.5, bf16[1,16384,512]{2,1,0:T(8,128)(2,1)} %param.4), kind=kLoop, calls=%fused_computation.5 | loop fusion | flops 67108864 | bytes 50331648 | tf_op jit(solution)/shard_map/convert_element_type | solution.py:41
  143.1 38.3 %all-gather.5.cloned.1.call-done = bf16[64,256,256]{2,1,0:T(8,128)(2,1)} async-done(((bf16[64,64,256]{2,1,0:T(8,128)(2,1)}), bf16[64,256,256]{2,1,0:T(8,128)(2,1)}) %all-gather.5.cloned.1.call-update) | async-done | bytes 8388624 | tf_op jit(solution)/shard_map/all_gather | solution.py:16
  181.5 16.4 %convert_bitcast_fusion = bf16[1,256,64,512]{1,3,2,0:T(8,128)(2,1)} fusion(bf16[64,256,512]{2,1,0:T(8,128)(2,1)} %bitcast.47, bf16[64,256,256]{2,1,0:T(8,128)(2,1)} %all-gather.5.cloned.1.call-done), kind=kOutput, calls=%fused_computation.18 | convolution fusion | flops 4303355904 | bytes 41943040 | tf_op jit(solution)/shard_map/jik,bjic->bkjc/dot_general | solution.py:47
  197.9 23.4 %copy.23 = bf16[1,256,64,512]{3,2,0,1:T(8,128)(2,1)} copy(bf16[1,256,64,512]{1,3,2,0:T(8,128)(2,1)} %convert_bitcast_fusion) | data formatting | bytes 33554432 | tf_op jit(solution)/shard_map/convert_element_type | solution.py:49
  221.3 262.6 %all-to-all-done = bf16[1,64,256,512]{3,1,0,2:T(8,128)(2,1)} async-done(((bf16[1,64,256,512]{3,1,0,2:T(8,128)(2,1)}), bf16[1,64,256,512]{3,1,0,2:T(8,128)(2,1)}, u32[]{:S(2)}, u32[]{:S(2)}) %all-to-all-start) | async-done | bytes 16777248 | tf_op jit(solution)/shard_map/all_to_all | solution.py:30
  483.8 7.1 all-to-all-start.1
  490.9 0.2 reduce-scatter.5.cloned.1.call-start
  491.2 12.1 %copy.20 = bf16[1,64,256,512]{3,2,1,0:T(8,128)(2,1)S(1)} copy(bf16[1,64,256,512]{3,1,0,2:T(8,128)(2,1)} %all-to-all-done) | data formatting | bytes 33554432 | tf_op jit(solution)/shard_map/all_to_all | solution.py:30
  503.3 21.2 %copy.21 = bf16[1,4,64,64,512]{4,2,1,3,0:T(8,128)(2,1)} copy(bf16[1,4,64,64,512]{4,3,1,2,0:T(8,128)(2,1)S(1)} %bitcast.53) | data formatting | bytes 33554432 | tf_op jit(solution)/shard_map/all_to_all | solution.py:30
  524.5 15.5 %multiply_convert_fusion = bf16[64,256,256]{2,1,0:T(8,128)(2,1)} fusion(bf16[64,256,512]{2,1,0:T(8,128)(2,1)} %bitcast.48, bf16[256,64,512]{2,0,1:T(8,128)(2,1)} %bitcast.49), kind=kOutput, calls=%fused_computation.16 | convolution fusion | flops 4303355904 | bytes 41943040 | tf_op jit(solution)/shard_map/bjic,bkjc->jik/dot_general | solution.py:44
  540.0 0.0 reduce-scatter.5.cloned.1.call-update
  540.0 0.3 reduce-scatter.3.cloned.1.call-start
  540.3 313.4 %all-to-all-done.1 = bf16[1,256,64,512]{3,2,0,1:T(8,128)(2,1)} async-done(((bf16[1,256,64,512]{3,2,0,1:T(8,128)(2,1)}), bf16[1,256,64,512]{3,2,0,1:T(8,128)(2,1)}, u32[]{:S(2)}, u32[]{:S(2)}) %all-to-all-start.1) | async-done | bytes 16777248 | tf_op jit(solution)/shard_map/all_to_all | solution.py:50
  853.7 14.1 %copy.24 = bf16[1,64,4,64,512]{4,3,2,1,0:T(8,128)(2,1)} copy(bf16[1,64,4,64,512]{4,3,1,2,0:T(8,128)(2,1)} %bitcast.13) | data formatting | bytes 33554432 | tf_op jit(solution)/shard_map/all_to_all | solution.py:50
  867.7 15.5 %multiply_convert_fusion.1 = bf16[64,256,256]{2,1,0:T(8,128)(2,1)} fusion(bf16[64,256,512]{2,1,0:T(8,128)(2,1)} %bitcast.51, bf16[64,256,512]{2,1,0:T(8,128)(2,1)} %bitcast.46), kind=kOutput, calls=%fused_computation.17 | convolution fusion | flops 4303355904 | bytes 41943040 | tf_op jit(solution)/shard_map/bijc,bikc->ijk/dot_general | solution.py:51
  883.2 0.0 reduce-scatter.3.cloned.1.call-update
  883.2 23.1 %fusion.10 = f32[64,512,256]{1,2,0:T(8,128)} fusion(bf16[64,256,512]{2,1,0:T(8,128)(2,1)} %bitcast.52, bf16[64,256,256]{2,1,0:T(8,128)(2,1)} %all-gather.3.cloned.1.call-done), kind=kOutput, calls=%fused_computation.20 | convolution fusion | flops 4294967296 | bytes 58720256 | tf_op jit(solution)/shard_map/ijk,bijc->bikc/dot_general | solution.py:54
  906.4 18.3 %fusion.11 = f32[64,512,256]{1,2,0:T(8,128)} fusion(bf16[64,256,256]{2,1,0:T(8,128)(2,1)} %all-gather.5.cloned.1.call-done, bf16[256,64,512]{2,0,1:T(8,128)(2,1)} %bitcast.50), kind=kOutput, calls=%fused_computation.21 | convolution fusion | flops 4294967296 | bytes 58720256 | tf_op jit(solution)/shard_map/jik,bkjc->bjic/dot_general | solution.py:31
  924.7 45.3 %fusion.3 = (bf16[1,16384,512]{2,1,0:T(8,128)(2,1)}, bf16[1,16384,512]{2,1,0:T(8,128)(2,1)}) fusion(bf16[1,16384,512]{2,1,0:T(8,128)(2,1)} %param.5, bf16[1,16384,512]{2,1,0:T(8,128)(2,1)} %param.4, f32[64,512,256]{1,2,0:T(8,128)} %fusion.10, f32[64,512,256]{1,2,0:T(8,128)} %fusion.11), kind=kLoop, calls=%fused_computation.8 | loop fusion | flops 134217728 | bytes 134217728 | tf_op jit(solution)/shard_map/convert_element_type | solution.py:59
  970.0 0.0 reduce-scatter.5.cloned.1.call-done
  970.0 0.0 reduce-scatter.3.cloned.1.call-done
Async XLA Ops:
  7.2 63.4 %all-gather.3.cloned.1.call-start = ((), (), s32[]{:S(2)}) async-start(), calls=%async_computation.4 | async-start | bytes 10485760 | tf_op jit(solution)/shard_map/all_gather | solution.py:15
  113.3 370.5 %all-to-all-start = ((bf16[1,64,256,512]{3,1,0,2:T(8,128)(2,1)}), bf16[1,64,256,512]{3,1,0,2:T(8,128)(2,1)}, u32[]{:S(2)}, u32[]{:S(2)}) async-start(bf16[1,64,256,512]{3,1,0,2:T(8,128)(2,1)} %copy.19), calls=%async_computation | async-start | bytes 33554432 | tf_op jit(solution)/shard_map/all_to_all | solution.py:30
  120.3 61.2 %all-gather.5.cloned.1.call-start = ((), (), s32[]{:S(2)}) async-start(), calls=%async_computation.5 | async-start | bytes 10485760 | tf_op jit(solution)/shard_map/all_gather | solution.py:16
  483.8 369.8 %all-to-all-start.1 = ((bf16[1,256,64,512]{3,2,0,1:T(8,128)(2,1)}), bf16[1,256,64,512]{3,2,0,1:T(8,128)(2,1)}, u32[]{:S(2)}, u32[]{:S(2)}) async-start(bf16[1,256,64,512]{3,2,0,1:T(8,128)(2,1)} %copy.23), calls=%async_computation.1 | async-start | bytes 33554432 | tf_op jit(solution)/shard_map/all_to_all | solution.py:50
  490.9 479.1 %reduce-scatter.5.cloned.1.call-start = ((), (), s32[]{:S(2)}) async-start(), calls=%async_computation.7 | async-start | bytes 10485760 | tf_op jit(solution)/shard_map/reduce_scatter | solution.py:64
  540.0 430.0 %reduce-scatter.3.cloned.1.call-start = ((), (), s32[]{:S(2)}) async-start(), calls=%async_computation.6 | async-start | bytes 10485760 | tf_op jit(solution)/shard_map/reduce_scatter | solution.py:61
Sparse Core Ops, SparseCore 0:
  9.6 60.9 all-gather.2
  122.7 58.7 all-gather.4
  540.2 71.9 reduce-scatter.4
  883.4 69.8 reduce-scatter.2
where the time goes:
time: 978 us; the launch traced here: 977 us
  waiting for transfers between devices  678 us (69%)
  matrix products  108 us (11%)
  local copies, waits for them, and re-layouts  94.3 us (10%)
  other arithmetic  67.4 us (7%)
  starting transfers between devices  14.6 us (1%)
  between operations  13.8 us (1%)
    all_to_all x1, waiting for transfers between devices, shards(): lax.all_to_all(back_sent, 'seq', split_axis=1, concat_axis=2, tiled=True)  313 us
    all_to_all x1, waiting for transfers between devices, shards(): lax.all_to_all(first_out, 'seq', split_axis=2, concat_axis=1, tiled=True)  263 us
    all_gather x1, waiting for transfers between devices, shards(): lax.all_gather(first_factor, 'dp', axis=1, tiled=True)  62.7 us
    convert_element_type x1, other arithmetic, shards(): input_grad = (local_grad.reshape(seqs_here, rows_here, channels) + cot_f3...  45.3 us
    all_gather x1, waiting for transfers between devices, shards(): lax.all_gather(second_factor, 'dp', axis=1, tiled=True)  38.3 us
    all_to_all x2, local copies, waits for them, and re-layouts, shards(): lax.all_to_all(first_out, 'seq', split_axis=2, concat_axis=1, tiled=True)  33.4 us
    convert_element_type x1, local copies, waits for them, and re-layouts, shards(): first_out = jnp.einsum('ijk,bikc->bijc', first_full, blocked, preferred_e...  23.4 us
    convert_element_type x1, local copies, waits for them, and re-layouts, shards(): back_sent = jnp.einsum('jik,bjic->bkjc', second_full, gated_cot, preferre...  23.4 us
  transfers between devices with their start and end apart: 6, of which 4 were waited for; matrix products, arithmetic and copies ran while one was open for 23% of the time, Pallas kernels for 0%

commit v1 on v0

--- a/solution.py
+++ b/solution.py
@@ -3,6 +3,33 @@
 import jax.numpy as jnp
 from jax import lax
 from jax.sharding import PartitionSpec as P
+from jax.lax import axis_index, axis_size, ppermute
+
+
+def cut_the_axis_part(frame):
+    y = axis_size("dp")
+    v_next, tile_out, mid_arr = (y, axis_index("dp"), frame.shape[1])
+    steps_seen = []
+    for pp in [*range(v_next)]:
+        steps_seen.append((pp, (pp + 1) % v_next))
+    block_list = []
+    for pp in tuple(range(v_next)):
+        block_list.append((pp, (pp - 1) % v_next))
+    all_values = jnp.zeros((*frame.shape[:1], v_next * mid_arr, *frame.shape[2:]), frame.dtype)
+    all_values = lax.dynamic_update_slice_in_dim(all_values, frame, tile_out * mid_arr, axis=1)
+    then = taken_in = frame
+    inter = v_next // 2
+    for src_i in [*range(1, inter + 1)]:
+        then = ppermute(then, "dp", steps_seen)
+        all_values = lax.dynamic_update_slice_in_dim(
+            all_values, then, (tile_out - src_i) % v_next * mid_arr, axis=1
+        )
+        if src_i < v_next - inter:
+            taken_in = ppermute(taken_in, "dp", block_list)
+            all_values = lax.dynamic_update_slice_in_dim(
+                all_values, taken_in, (tile_out + src_i) % v_next * mid_arr, axis=1
+            )
+    return all_values
 
 
 def silu_parts(values):
@@ -13,7 +40,7 @@
 def shards(inputs, cotangent, first_factor, second_factor):
     first_full, second_full = (
         lax.all_gather(first_factor, "dp", axis=1, tiled=True),
-        lax.all_gather(second_factor, "dp", axis=1, tiled=True),
+        cut_the_axis_part(second_factor),
     )
     seqs_here = inputs.shape[0]
     rows_here = inputs.shape[1]

time: 978 us -> 1010 us (1.033)
  waiting for transfers between devices: 678 us -> 699 us
    all_to_all x1, waiting for transfers between devices: 263 us -> 334 us  [shards(): lax.all_to_all(first_out, 'seq', split_axis=2, concat_axis=1, tiled=True)]
    all_to_all x1, waiting for transfers between devices: 313 us -> 258 us  [shards(): lax.all_to_all(back_sent, 'seq', split_axis=1, concat_axis=2, tiled=True)]
    ppermute x0 -> x3, waiting for transfers between devices: none -> 43.8 us  [the longest x2 43.8 us: cut_the_axis_part(): then = ppermute(then, 'dp', steps_seen)]
    all_gather x1 -> x0, waiting for transfers between devices: 38.3 us -> none  [shards(): lax.all_gather(second_factor, 'dp', axis=1, tiled=True)]
  transfers between devices with their start and end apart: 6 -> 8, of which waited for: 4 -> 4; matrix products, arithmetic and copies ran while one was open for 23% -> 23% of each run, Pallas kernels for 0% -> 0%
where the time goes in v1:
time: 1010 us
  waiting for transfers between devices  699 us (69%)
  matrix products  107 us (11%)
  local copies, waits for them, and re-layouts  104 us (10%)
  other arithmetic  66.4 us (7%)
  starting transfers between devices  19.4 us (2%)
  between operations  13.9 us (1%)
    all_to_all x1, waiting for transfers between devices, shards(): lax.all_to_all(first_out, 'seq', split_axis=2, concat_axis=1, tiled=True)  334 us
    all_to_all x1, waiting for transfers between devices, shards(): lax.all_to_all(back_sent, 'seq', split_axis=1, concat_axis=2, tiled=True)  258 us
    all_gather x1, waiting for transfers between devices, shards(): lax.all_gather(first_factor, 'dp', axis=1, tiled=True)  61.7 us
    convert_element_type x1, other arithmetic, shards(): input_grad = (local_grad.reshape(seqs_here, rows_here, channels) + cot_f3...  45.2 us
    ppermute x2, waiting for transfers between devices, cut_the_axis_part(): then = ppermute(then, 'dp', steps_seen)  43.8 us
    all_to_all x2, local copies, waits for them, and re-layouts, shards(): lax.all_to_all(first_out, 'seq', split_axis=2, concat_axis=1, tiled=True)  33.3 us
    dot_general x1, matrix products, shards(): jnp.einsum('ijk,bijc->bikc', first_full, back_rows, preferred_element_typ...  23.5 us
    convert_element_type x1, local copies, waits for them, and re-layouts, shards(): first_out = jnp.einsum('ijk,bikc->bijc', first_full, blocked, preferred_e...  23.3 us
  transfers between devices with their start and end apart: 8, of which 4 were waited for; matrix products, arithmetic and copies ran while one was open for 23% of the time, Pallas kernels for 0%

profile of v1, /device:TPU:0, one launch (start us, length us, event | category | flops | bytes accessed | tf_op | source)
XLA Modules:
  0.0 1009.9 jit_solution(7565920386471684931)
XLA Ops:
  7.2 0.5 collective-permute-start
  7.7 2.0 collective-permute-start.1
  9.7 43.8 %collective-permute-done = bf16[64,64,256]{2,1,0:T(8,128)(2,1)} collective-permute-done((bf16[64,64,256]{2,1,0:T(8,128)(2,1)}, bf16[64,64,256]{2,1,0:T(8,128)(2,1)}, u32[]{:S(2)}, u32[]{:S(2)}) %collective-permute-start) | collective-permute-done | bytes 2097184 | tf_op jit(solution)/shard_map/ppermute | solution.py:23
  53.5 2.5 collective-permute-start.2
  56.0 21.2 %fusion = bf16[1,16384,512]{2,1,0:T(8,128)(2,1)} fusion(bf16[1,16384,512]{2,1,0:T(8,128)(2,1)} %param.5, bf16[1,16384,512]{2,1,0:T(8,128)(2,1)} %param.4), kind=kLoop, calls=%fused_computation.5 | loop fusion | flops 67108864 | bytes 50331648 | tf_op jit(solution)/shard_map/convert_element_type | solution.py:68
  77.2 1.0 broadcast_in_dim.3
  78.2 0.3 constant_dynamic-update-slice_fusion.3
  78.5 1.9 constant_dynamic-update-slice_fusion.2
  80.4 1.9 constant_dynamic-update-slice_fusion.1
  82.3 1.9 constant_dynamic-update-slice_fusion
  84.2 3.2 copy-done
  87.5 14.8 %convert_bitcast_fusion = bf16[1,256,64,512]{1,3,2,0:T(8,128)(2,1)} fusion(bf16[64,256,512]{2,1,0:T(8,128)(2,1)} %bitcast.47, bf16[64,256,256]{2,1,0:T(8,128)(2,1)S(1)} %constant_dynamic-update-slice_fusion), kind=kOutput, calls=%fused_computation.18 | convolution fusion | flops 4303355904 | bytes 41943040 | tf_op jit(solution)/shard_map/jik,bjic->bkjc/dot_general | solution.py:74
  102.3 23.2 %copy.23 = bf16[1,256,64,512]{3,2,0,1:T(8,128)(2,1)} copy(bf16[1,256,64,512]{1,3,2,0:T(8,128)(2,1)} %convert_bitcast_fusion) | data formatting | bytes 33554432 | tf_op jit(solution)/shard_map/convert_element_type | solution.py:76
  125.5 7.0 all-to-all-start.1
  132.5 0.0 all-gather.2.cloned.1.call-start
  132.5 0.7 all-gather.2.cloned.1.call-update
  133.2 61.7 %all-gather.2.cloned.1.call-done = bf16[64,256,256]{2,1,0:T(8,128)(2,1)} async-done(((bf16[64,64,256]{2,1,0:T(8,128)(2,1)}), bf16[64,256,256]{2,1,0:T(8,128)(2,1)}) %all-gather.2.cloned.1.call-update) | async-done | bytes 8388624 | tf_op jit(solution)/shard_map/all_gather | solution.py:42
  194.9 19.3 %convert_bitcast_fusion.1 = bf16[1,64,256,512]{2,3,1,0:T(8,128)(2,1)} fusion(bf16[64,256,512]{2,1,0:T(8,128)(2,1)} %bitcast.45, bf16[64,256,256]{2,1,0:T(8,128)(2,1)} %all-gather.2.cloned.1.call-done), kind=kOutput, calls=%fused_computation.19 | convolution fusion | flops 4303355904 | bytes 41943040 | tf_op jit(solution)/shard_map/ijk,bikc->bijc/dot_general | solution.py:54
  214.2 23.3 %copy.19 = bf16[1,64,256,512]{3,1,0,2:T(8,128)(2,1)} copy(bf16[1,64,256,512]{2,3,1,0:T(8,128)(2,1)} %convert_bitcast_fusion.1) | data formatting | bytes 33554432 | tf_op jit(solution)/shard_map/convert_element_type | solution.py:56
  237.5 258.2 %all-to-all-done.1 = bf16[1,256,64,512]{3,2,0,1:T(8,128)(2,1)} async-done(((bf16[1,256,64,512]{3,2,0,1:T(8,128)(2,1)}), bf16[1,256,64,512]{3,2,0,1:T(8,128)(2,1)}, u32[]{:S(2)}, u32[]{:S(2)}) %all-to-all-start.1) | async-done | bytes 16777248 | tf_op jit(solution)/shard_map/all_to_all | solution.py:77
  495.7 7.1 all-to-all-start
  502.8 0.0 reduce-scatter.3.cloned.1.call-start
  502.8 14.1 %copy.24 = bf16[1,64,4,64,512]{4,3,2,1,0:T(8,128)(2,1)} copy(bf16[1,64,4,64,512]{4,3,1,2,0:T(8,128)(2,1)} %bitcast.13) | data formatting | bytes 33554432 | tf_op jit(solution)/shard_map/all_to_all | solution.py:77
  516.9 15.5 %multiply_convert_fusion.1 = bf16[64,256,256]{2,1,0:T(8,128)(2,1)} fusion(bf16[64,256,512]{2,1,0:T(8,128)(2,1)} %bitcast.49, bf16[64,256,512]{2,1,0:T(8,128)(2,1)} %bitcast.46), kind=kOutput, calls=%fused_computation.17 | convolution fusion | flops 4303355904 | bytes 41943040 | tf_op jit(solution)/shard_map/bijc,bikc->ijk/dot_general | solution.py:78
  532.4 0.2 reduce-scatter.5.cloned.1.call-start
  532.6 334.3 %all-to-all-done = bf16[1,64,256,512]{3,1,0,2:T(8,128)(2,1)} async-done(((bf16[1,64,256,512]{3,1,0,2:T(8,128)(2,1)}), bf16[1,64,256,512]{3,1,0,2:T(8,128)(2,1)}, u32[]{:S(2)}, u32[]{:S(2)}) %all-to-all-start) | async-done | bytes 16777248 | tf_op jit(solution)/shard_map/all_to_all | solution.py:57
  867.0 12.1 %copy.20 = bf16[1,64,256,512]{3,2,1,0:T(8,128)(2,1)S(1)} copy(bf16[1,64,256,512]{3,1,0,2:T(8,128)(2,1)} %all-to-all-done) | data formatting | bytes 33554432 | tf_op jit(solution)/shard_map/all_to_all | solution.py:57
  879.1 21.2 %copy.21 = bf16[1,4,64,64,512]{4,2,1,3,0:T(8,128)(2,1)} copy(bf16[1,4,64,64,512]{4,3,1,2,0:T(8,128)(2,1)S(1)} %bitcast.53) | data formatting | bytes 33554432 | tf_op jit(solution)/shard_map/all_to_all | solution.py:57
  900.3 15.5 %multiply_convert_fusion = bf16[64,256,256]{2,1,0:T(8,128)(2,1)} fusion(bf16[64,256,512]{2,1,0:T(8,128)(2,1)} %bitcast.48, bf16[256,64,512]{2,0,1:T(8,128)(2,1)} %bitcast.51), kind=kOutput, calls=%fused_computation.16 | convolution fusion | flops 4303355904 | bytes 41943040 | tf_op jit(solution)/shard_map/bjic,bkjc->jik/dot_general | solution.py:71
  915.9 23.5 %fusion.10 = f32[64,512,256]{1,2,0:T(8,128)} fusion(bf16[64,256,512]{2,1,0:T(8,128)(2,1)} %bitcast.50, bf16[64,256,256]{2,1,0:T(8,128)(2,1)} %all-gather.2.cloned.1.call-done), kind=kOutput, calls=%fused_computation.24 | convolution fusion | flops 4294967296 | bytes 58720256 | tf_op jit(solution)/shard_map/ijk,bijc->bikc/dot_general | solution.py:81
  939.4 18.7 %fusion.11 = f32[64,512,256]{1,2,0:T(8,128)} fusion(bf16[64,256,256]{2,1,0:T(8,128)(2,1)} %copy-done, bf16[256,64,512]{2,0,1:T(8,128)(2,1)} %bitcast.52), kind=kOutput, calls=%fused_computation.25 | convolution fusion | flops 4294967296 | bytes 58720256 | tf_op jit(solution)/shard_map/jik,bkjc->bjic/dot_general | solution.py:58
  958.1 45.2 %fusion.3 = (bf16[1,16384,512]{2,1,0:T(8,128)(2,1)}, bf16[1,16384,512]{2,1,0:T(8,128)(2,1)}) fusion(bf16[1,16384,512]{2,1,0:T(8,128)(2,1)} %param.5, bf16[1,16384,512]{2,1,0:T(8,128)(2,1)} %param.4, f32[64,512,256]{1,2,0:T(8,128)} %fusion.10, f32[64,512,256]{1,2,0:T(8,128)} %fusion.11), kind=kLoop, calls=%fused_computation.8 | loop fusion | flops 134217728 | bytes 134217728 | tf_op jit(solution)/shard_map/convert_element_type | solution.py:86
  (9 shorter events, 0.1 us)
Async XLA Ops:
  7.2 71.0 %copy-start.1 = (bf16[64,64,256]{2,1,0:T(8,128)(2,1)S(1)}, bf16[64,64,256]{2,1,0:T(8,128)(2,1)}, u32[]{:S(2)}) copy-start(bf16[64,64,256]{2,1,0:T(8,128)(2,1)} %param.7) | copy-start | bytes 6291460
  7.2 46.3 %collective-permute-start = (bf16[64,64,256]{2,1,0:T(8,128)(2,1)}, bf16[64,64,256]{2,1,0:T(8,128)(2,1)}, u32[]{:S(2)}, u32[]{:S(2)}) collective-permute-start(bf16[64,64,256]{2,1,0:T(8,128)(2,1)} %param.7), channel_id=1, source_target_pairs={{0,1},{1,2},{2,3},{3,0},{4,5},{5,6},{6,7},{7,4},{8,9},{9,10},{10,1... | collective-permute-start | bytes 6291464 | tf_op jit(solution)/shard_map/ppermute | solution.py:23
  7.7 72.7 %collective-permute-start.1 = (bf16[64,64,256]{2,1,0:T(8,128)(2,1)}, bf16[64,64,256]{2,1,0:T(8,128)(2,1)}, u32[]{:S(2)}, u32[]{:S(2)}) collective-permute-start(bf16[64,64,256]{2,1,0:T(8,128)(2,1)} %param.7), channel_id=1, source_target_pairs={{0,3},{1,0},{2,1},{3,2},{4,7},{5,4},{6,5},{7,6},{8,11},{9,8},{10,9... | collective-permute-start | bytes 6291464 | tf_op jit(solution)/shard_map/ppermute | solution.py:28
  53.5 28.9 %collective-permute-start.2 = (bf16[64,64,256]{2,1,0:T(8,128)(2,1)}, bf16[64,64,256]{2,1,0:T(8,128)(2,1)}, u32[]{:S(2)}, u32[]{:S(2)}) collective-permute-start(bf16[64,64,256]{2,1,0:T(8,128)(2,1)} %collective-permute-done), channel_id=1, source_target_pairs={{0,1},{1,2},{2,3},{3,0},{4,5},{5,6},{6,7},{7,4},{8,9},{9,10},{10,1... | collective-permute-start | bytes 6291464 | tf_op jit(solution)/shard_map/ppermute | solution.py:23
  84.2 3.2 copy-start
  125.5 370.2 %all-to-all-start.1 = ((bf16[1,256,64,512]{3,2,0,1:T(8,128)(2,1)}), bf16[1,256,64,512]{3,2,0,1:T(8,128)(2,1)}, u32[]{:S(2)}, u32[]{:S(2)}) async-start(bf16[1,256,64,512]{3,2,0,1:T(8,128)(2,1)} %copy.23), calls=%async_computation.1 | async-start | bytes 33554432 | tf_op jit(solution)/shard_map/all_to_all | solution.py:77
  132.5 62.4 %all-gather.2.cloned.1.call-start = ((), (), s32[]{:S(2)}) async-start(), calls=%async_computation.4 | async-start | bytes 10485760 | tf_op jit(solution)/shard_map/all_gather | solution.py:42
  495.7 371.3 %all-to-all-start = ((bf16[1,64,256,512]{3,1,0,2:T(8,128)(2,1)}), bf16[1,64,256,512]{3,1,0,2:T(8,128)(2,1)}, u32[]{:S(2)}, u32[]{:S(2)}) async-start(bf16[1,64,256,512]{3,1,0,2:T(8,128)(2,1)} %copy.19), calls=%async_computation | async-start | bytes 33554432 | tf_op jit(solution)/shard_map/all_to_all | solution.py:57
  502.8 500.5 %reduce-scatter.3.cloned.1.call-start = ((), (), s32[]{:S(2)}) async-start(), calls=%async_computation.5 | async-start | bytes 10485760 | tf_op jit(solution)/shard_map/reduce_scatter | solution.py:88
  532.4 470.9 %reduce-scatter.5.cloned.1.call-start = ((), (), s32[]{:S(2)}) async-start(), calls=%async_computation.6 | async-start | bytes 10485760 | tf_op jit(solution)/shard_map/reduce_scatter | solution.py:91
Sparse Core Ops, SparseCore 0:
  134.9 59.9 all-gather.1
  532.5 72.9 reduce-scatter.2
  916.0 69.1 reduce-scatter.4
